TPU v7x, 256 devices: a whole 4x4x8 slice. The times are simulated.
256 devices in a mesh: pool: 32 (over y, z), blk: 8 (over x, core).
Axes of the slice: x: 4, y: 4, z: 8, core: 2. Of those that a mesh axis runs over, the one named last changes fastest.
Arguments:
- queries: bfloat16 [32768, 4096], P(('pool', 'blk')), may hold values from -7.5 to 7.5
- span_kv: bfloat16 [32768, 1024], P(('pool', 'blk')), may hold values from -6 to 6
- kv_store: bfloat16 [512, 64, 1024], P('pool'), may hold values from -6 to 6
- page_ids: int32 [32, 32], P('pool'), may hold values from 0 to 15
- page_owner: int32 [32, 32], P('pool'), may hold values from 0 to 31, as said below
- prefix_len: int32 [32], P('pool'), may hold values from 1280 to 2048, as said below
Outputs:
- attended: bfloat16 [32768, 4096], P(('pool', 'blk'))
Inputs may be any that keep to these rules, and one draw needn't show every extreme that they name: `page_owner`: each request's list names 16 owners, each exactly 2 times; one owner is named by every request. `prefix_len`: some request has a prefix of exactly 2048 tokens.
All inputs are finite; a program needn't handle non-finite values.
Results may differ from a plain program's by a relative error of at most 0.005.
Values may be sent and summed in bfloat16 or wider, within the bound.
A program may use at most 128 MiB of HBM per device.

v0:
```python
import math

import jax
import jax.numpy as jnp
from jax import lax
from jax.sharding import PartitionSpec as P

QH = 32
KVH = 4
DH = 128
PAGE = 64
CAP = 2
GROUP = 8


def attend_block(state, queries_four, pairs_in, usable):
    running, denom_sum, numer = state
    rows_in = pairs_in.shape[0]
    pairs = pairs_in.reshape(rows_in, 2, KVH, DH)
    scores = jnp.einsum(
        "qgjd,ngd->qgjn", queries_four, pairs[:, 0], preferred_element_type=jnp.float32
    ) * (1.0 / math.sqrt(DH))
    allowed = usable[:, None, None, :]
    block_top = jnp.max(jnp.where(allowed, scores, -1e30), axis=-1)
    new_top = jnp.maximum(running, block_top)
    weights = jnp.where(allowed, jnp.exp(scores - new_top[..., None]), 0.0)
    factor = jnp.exp(running - new_top)
    denom_sum = denom_sum * factor + jnp.sum(weights, axis=-1)
    numer = numer * factor[..., None] + jnp.einsum(
        "qgjn,ngd->qgjd",
        weights.astype(jnp.bfloat16),
        pairs[:, 1],
        preferred_element_type=jnp.float32,
    )
    return (new_top, denom_sum, numer)


def attend_rows(state, queries_four, pairs_in, usable):
    rows_in = pairs_in.shape[0]
    block_len = 512
    blocks = rows_in // block_len
    lead = usable.shape[0]
    pair_blocks = pairs_in.reshape(blocks, block_len, pairs_in.shape[1])
    usable_blocks = usable.reshape(lead, blocks, block_len).transpose(1, 0, 2)

    def advance(inner, pieces):
        return (attend_block(inner, queries_four, pieces[0], pieces[1]), None)

    state, unused = lax.scan(advance, state, (pair_blocks, usable_blocks))
    return state


def per_device(queries, span_kv, kv_store, page_ids, page_owner, prefix_len):
    pools = lax.axis_size("pool")
    place = lax.axis_index("blk")
    q_rows = queries.shape[0]
    feats = kv_store.shape[2]
    queries_four = queries.reshape(q_rows, KVH, GROUP, DH)
    owners = page_owner[0]
    ident = page_ids[0]
    limit = prefix_len[0]
    listed = owners.shape[0]
    order = jnp.arange(listed, dtype=jnp.int32)
    same_owner = owners[:, None] == owners[None, :]
    earlier = order[None, :] < order[:, None]
    rank_in = jnp.sum((same_owner & earlier).astype(jnp.int32), axis=1)
    owner_grid = jnp.arange(pools, dtype=jnp.int32)[:, None, None]
    slot_grid = jnp.arange(CAP, dtype=jnp.int32)[None, :, None]
    hits = ((owners[None, None, :] == owner_grid) & (rank_in[None, None, :] == slot_grid)).astype(
        jnp.int32
    )
    slot_page = jnp.sum(hits * ident[None, None, :], axis=2)
    slot_first = jnp.sum(hits * order[None, None, :], axis=2)
    slot_live = jnp.sum(hits, axis=2)
    share = PAGE
    pages = kv_store[lax.all_to_all(slot_page, "pool", split_axis=0, concat_axis=0, tiled=True)]
    fetched = lax.all_to_all(pages, "pool", split_axis=0, concat_axis=0, tiled=True)
    shard_len = pools * CAP * share
    flat_pages = fetched.reshape(shard_len, feats)
    page_start = slot_first.reshape(-1) * PAGE
    page_live = slot_live.reshape(-1)
    slot_count = pools * CAP
    state = (
        jnp.full((q_rows, KVH, GROUP), -1e30, jnp.float32),
        jnp.zeros((q_rows, KVH, GROUP), jnp.float32),
        jnp.zeros((q_rows, KVH, GROUP, DH), jnp.float32),
    )
    index = jnp.arange(shard_len, dtype=jnp.int32)
    source = index // shard_len
    within = index % shard_len
    slot = within // share
    column = within % share
    matched = slot[:, None] == jnp.arange(slot_count, dtype=jnp.int32)[None, :]
    first = jnp.sum(jnp.where(matched, page_start[None, :], 0), axis=1)
    living = jnp.sum(jnp.where(matched, page_live[None, :], 0), axis=1)
    position = first + source * share + column
    state = attend_rows(
        state, queries_four, flat_pages, ((living > 0) & (position < limit))[None, :]
    )
    query_pos = place * q_rows + jnp.arange(q_rows, dtype=jnp.int32)
    piece = lax.all_gather(span_kv, "blk", axis=0, tiled=True)
    key_pos = jnp.arange(piece.shape[0], dtype=jnp.int32)
    state = attend_rows(state, queries_four, piece, key_pos[None, :] <= query_pos[:, None])
    running, denom_sum, numer = state
    return (numer / denom_sum[..., None]).astype(jnp.bfloat16).reshape(q_rows, QH * DH)


def solution(mesh):
    in_specs = (
        P(("pool", "blk"), None),
        P(("pool", "blk"), None),
        P("pool", None, None),
        P("pool", None),
        P("pool", None),
        P("pool"),
    )
    out_specs = P(("pool", "blk"), None)
    return jax.shard_map(
        per_device, mesh=mesh, in_specs=in_specs, out_specs=out_specs, check_vma=False
    )
```

profile of v0, /device:TPU:1, one launch (start us, length us, event | category | flops | bytes accessed | tf_op | source)
XLA Modules:
  0.0 432.6 jit_solution(13128077996819959735)
XLA Ops:
  9.2 20.5 %all_to_all.17 = s32[32,1,2]{2,1,0:T(1,128)S(1)} all-to-all(s32[32,1,2]{2,1,0:T(1,128)S(1)} %copy.55), channel_id=1, replica_groups=mesh['pool'=32,'blk'=8] {'pool'}, dimensions={0} | all-to-all | bytes 512 | tf_op jit(solution)/shard_map/all_to_all | solution.py:76
  30.0 5.4 %gather_fusion = bf16[64,64,1024]{2,1,0:T(8,128)(2,1)} fusion(bf16[16,64,1024]{2,1,0:T(8,128)(2,1)S(1)} %copy-done, s32[1024]{0:T(1024)S(1)} %pad_clamp_fusion), kind=kCustom, calls=%fused_computation | custom fusion | bytes 16777472 | tf_op jit(solution)/shard_map/gather | solution.py:76
  35.4 5.1 %all-to-all-start.1 = ((bf16[32,2,64,1024]{3,2,1,0:T(8,128)(2,1)}), bf16[32,2,64,1024]{3,2,1,0:T(8,128)(2,1)}, u32[]{:S(2)}, u32[]{:S(2)}) async-start(bf16[32,2,64,1024]{3,2,1,0:T(8,128)(2,1)} %bitcast.128), calls=%async_computation.1 | async-start | bytes 16777216 | tf_op jit(solution)/shard_map/all_to_all | solution.py:77
  46.1 179.0 %all-to-all-done.1 = bf16[32,2,64,1024]{3,2,1,0:T(8,128)(2,1)} async-done(((bf16[32,2,64,1024]{3,2,1,0:T(8,128)(2,1)}), bf16[32,2,64,1024]{3,2,1,0:T(8,128)(2,1)}, u32[]{:S(2)}, u32[]{:S(2)}) %all-to-all-start.1) | async-done | bytes 8388640 | tf_op jit(solution)/shard_map/all_to_all | solution.py:77
  225.1 172.2 %while.30 = (s32[]{:T(128)}, f32[128,4,8]{0,2,1:T(8,128)S(1)}, f32[128,4,8]{0,2,1:T(8,128)S(1)}, f32[128,4,8,128]{0,3,2,1:T(8,128)}, pred[8,1,512]{2,0,1:T(8,128...) while((s32[]{:T(128)}, f32[128,4,8]{0,2,1:T(8,128)S(1)}, ...), condition=%wide.region_9.10_spmd.clone, body=%wide.region_6.9_spmd.clone.sunk | while | flops 1098403840 | bytes 69470864 | solution.py:49
  229.7 6.2 %fusion.69 = (f32[128,4,8]{0,2,1:T(8,128)S(1)}, f32[4,512,128,8]{2,1,3,0:T(8,128)}) fusion(pred[512]{0:T(512)(128)(4,1)S(1)} %bitcast_reduce_fusion.2, bf16[128,4,8,128]{3,0,2,1:T(8,128)(2,1)S(1)} %get-tuple-element.334, bf16[512,2,4,128]{0,3,2,1:T(8,128)(2,1)} %bitcast.124), kind=kOutput, calls=%fused_computation.25.clone.1 | convolution fusion | flops 543158272 | bytes 9978368 | tf_op jit(solution)/shard_map/while/body/eval_jaxpr/qgjd,ngd->qgjn/dot_general | solution.py:20
  236.0 4.6 %fusion.70 = f32[128,4,8]{0,2,1:T(8,128)S(1)} fusion(f32[4,512,128,8]{2,1,3,0:T(8,128)} %get-tuple-element.307, f32[128,4,8]{0,2,1:T(8,128)S(1)} %select_maximum_fusion.2, pred[512]{0:T(512)(128)(4,1)S(1)} %bitcast_reduce_fusion.2), kind=kLoop, calls=%fused_computation.29.clone.1 | loop fusion | flops 8384512 | bytes 8421888 | tf_op jit(solution)/shard_map/while/body/eval_jaxpr/reduce_sum | solution.py:28
  250.6 6.2 %fusion.69 = (f32[128,4,8]{0,2,1:T(8,128)S(1)}, f32[4,512,128,8]{2,1,3,0:T(8,128)}) fusion(pred[512]{0:T(512)(128)(4,1)S(1)} %bitcast_reduce_fusion.2, bf16[128,4,8,128]{3,0,2,1:T(8,128)(2,1)S(1)} %get-tuple-element.334, bf16[512,2,4,128]{0,3,2,1:T(8,128)(2,1)} %bitcast.124), kind=kOutput, calls=%fused_computation.25.clone.1 | convolution fusion | flops 543158272 | bytes 9978368 | tf_op jit(solution)/shard_map/while/body/eval_jaxpr/qgjd,ngd->qgjn/dot_general | solution.py:20
  256.9 4.6 %fusion.70 = f32[128,4,8]{0,2,1:T(8,128)S(1)} fusion(f32[4,512,128,8]{2,1,3,0:T(8,128)} %get-tuple-element.307, f32[128,4,8]{0,2,1:T(8,128)S(1)} %select_maximum_fusion.2, pred[512]{0:T(512)(128)(4,1)S(1)} %bitcast_reduce_fusion.2), kind=kLoop, calls=%fused_computation.29.clone.1 | loop fusion | flops 8384512 | bytes 8421888 | tf_op jit(solution)/shard_map/while/body/eval_jaxpr/reduce_sum | solution.py:28
  262.7 4.9 %bitcast_add_fusion.5 = f32[128,4,8,128]{0,3,2,1:T(8,128)} fusion(f32[128,4,8,128]{0,3,2,1:T(8,128)} %get-tuple-element.322, f32[4,512,128,8]{2,1,3,0:T(8,128)S(1)} %copy-done.1, f32[128,4,8]{0,2,1:T(8,128)S(1)} %select_maximum_fusion.2, pred[512]{0:T(512)(128)(4,1)S(1)} %bitcast_reduce_fusion.2, f32[128,4,8]{0,2,1:T(8,128)S(1)} %get-tuple-element.309, ...), kind=kOutput, calls=%fused_computation.35.clone.1 | convolution fusion | flops 546832384 | bytes 13140481 | tf_op jit(solution)/shard_map/while/body/eval_jaxpr/qgjn,ngd->qgjd/dot_general | solution.py:29
  272.2 6.2 %fusion.69 = (f32[128,4,8]{0,2,1:T(8,128)S(1)}, f32[4,512,128,8]{2,1,3,0:T(8,128)}) fusion(pred[512]{0:T(512)(128)(4,1)S(1)} %bitcast_reduce_fusion.2, bf16[128,4,8,128]{3,0,2,1:T(8,128)(2,1)S(1)} %get-tuple-element.334, bf16[512,2,4,128]{0,3,2,1:T(8,128)(2,1)} %bitcast.124), kind=kOutput, calls=%fused_computation.25.clone.1 | convolution fusion | flops 543158272 | bytes 9978368 | tf_op jit(solution)/shard_map/while/body/eval_jaxpr/qgjd,ngd->qgjn/dot_general | solution.py:20
  284.3 4.9 %bitcast_add_fusion.5 = f32[128,4,8,128]{0,3,2,1:T(8,128)} fusion(f32[128,4,8,128]{0,3,2,1:T(8,128)} %get-tuple-element.322, f32[4,512,128,8]{2,1,3,0:T(8,128)S(1)} %copy-done.1, f32[128,4,8]{0,2,1:T(8,128)S(1)} %select_maximum_fusion.2, pred[512]{0:T(512)(128)(4,1)S(1)} %bitcast_reduce_fusion.2, f32[128,4,8]{0,2,1:T(8,128)S(1)} %get-tuple-element.309, ...), kind=kOutput, calls=%fused_computation.35.clone.1 | convolution fusion | flops 546832384 | bytes 13140481 | tf_op jit(solution)/shard_map/while/body/eval_jaxpr/qgjn,ngd->qgjd/dot_general | solution.py:29
  293.8 6.2 %fusion.69 = (f32[128,4,8]{0,2,1:T(8,128)S(1)}, f32[4,512,128,8]{2,1,3,0:T(8,128)}) fusion(pred[512]{0:T(512)(128)(4,1)S(1)} %bitcast_reduce_fusion.2, bf16[128,4,8,128]{3,0,2,1:T(8,128)(2,1)S(1)} %get-tuple-element.334, bf16[512,2,4,128]{0,3,2,1:T(8,128)(2,1)} %bitcast.124), kind=kOutput, calls=%fused_computation.25.clone.1 | convolution fusion | flops 543158272 | bytes 9978368 | tf_op jit(solution)/shard_map/while/body/eval_jaxpr/qgjd,ngd->qgjn/dot_general | solution.py:20
  305.9 4.9 %bitcast_add_fusion.5 = f32[128,4,8,128]{0,3,2,1:T(8,128)} fusion(f32[128,4,8,128]{0,3,2,1:T(8,128)} %get-tuple-element.322, f32[4,512,128,8]{2,1,3,0:T(8,128)S(1)} %copy-done.1, f32[128,4,8]{0,2,1:T(8,128)S(1)} %select_maximum_fusion.2, pred[512]{0:T(512)(128)(4,1)S(1)} %bitcast_reduce_fusion.2, f32[128,4,8]{0,2,1:T(8,128)S(1)} %get-tuple-element.309, ...), kind=kOutput, calls=%fused_computation.35.clone.1 | convolution fusion | flops 546832384 | bytes 13140481 | tf_op jit(solution)/shard_map/while/body/eval_jaxpr/qgjn,ngd->qgjd/dot_general | solution.py:29
  315.5 6.2 %fusion.69 = (f32[128,4,8]{0,2,1:T(8,128)S(1)}, f32[4,512,128,8]{2,1,3,0:T(8,128)}) fusion(pred[512]{0:T(512)(128)(4,1)S(1)} %bitcast_reduce_fusion.2, bf16[128,4,8,128]{3,0,2,1:T(8,128)(2,1)S(1)} %get-tuple-element.334, bf16[512,2,4,128]{0,3,2,1:T(8,128)(2,1)} %bitcast.124), kind=kOutput, calls=%fused_computation.25.clone.1 | convolution fusion | flops 543158272 | bytes 9978368 | tf_op jit(solution)/shard_map/while/body/eval_jaxpr/qgjd,ngd->qgjn/dot_general | solution.py:20
  327.5 4.9 %bitcast_add_fusion.5 = f32[128,4,8,128]{0,3,2,1:T(8,128)} fusion(f32[128,4,8,128]{0,3,2,1:T(8,128)} %get-tuple-element.322, f32[4,512,128,8]{2,1,3,0:T(8,128)S(1)} %copy-done.1, f32[128,4,8]{0,2,1:T(8,128)S(1)} %select_maximum_fusion.2, pred[512]{0:T(512)(128)(4,1)S(1)} %bitcast_reduce_fusion.2, f32[128,4,8]{0,2,1:T(8,128)S(1)} %get-tuple-element.309, ...), kind=kOutput, calls=%fused_computation.35.clone.1 | convolution fusion | flops 546832384 | bytes 13140481 | tf_op jit(solution)/shard_map/while/body/eval_jaxpr/qgjn,ngd->qgjd/dot_general | solution.py:29
  337.1 6.2 %fusion.69 = (f32[128,4,8]{0,2,1:T(8,128)S(1)}, f32[4,512,128,8]{2,1,3,0:T(8,128)}) fusion(pred[512]{0:T(512)(128)(4,1)S(1)} %bitcast_reduce_fusion.2, bf16[128,4,8,128]{3,0,2,1:T(8,128)(2,1)S(1)} %get-tuple-element.334, bf16[512,2,4,128]{0,3,2,1:T(8,128)(2,1)} %bitcast.124), kind=kOutput, calls=%fused_computation.25.clone.1 | convolution fusion | flops 543158272 | bytes 9978368 | tf_op jit(solution)/shard_map/while/body/eval_jaxpr/qgjd,ngd->qgjn/dot_general | solution.py:20
  349.2 4.9 %bitcast_add_fusion.5 = f32[128,4,8,128]{0,3,2,1:T(8,128)} fusion(f32[128,4,8,128]{0,3,2,1:T(8,128)} %get-tuple-element.322, f32[4,512,128,8]{2,1,3,0:T(8,128)S(1)} %copy-done.1, f32[128,4,8]{0,2,1:T(8,128)S(1)} %select_maximum_fusion.2, pred[512]{0:T(512)(128)(4,1)S(1)} %bitcast_reduce_fusion.2, f32[128,4,8]{0,2,1:T(8,128)S(1)} %get-tuple-element.309, ...), kind=kOutput, calls=%fused_computation.35.clone.1 | convolution fusion | flops 546832384 | bytes 13140481 | tf_op jit(solution)/shard_map/while/body/eval_jaxpr/qgjn,ngd->qgjd/dot_general | solution.py:29
  358.7 6.2 %fusion.69 = (f32[128,4,8]{0,2,1:T(8,128)S(1)}, f32[4,512,128,8]{2,1,3,0:T(8,128)}) fusion(pred[512]{0:T(512)(128)(4,1)S(1)} %bitcast_reduce_fusion.2, bf16[128,4,8,128]{3,0,2,1:T(8,128)(2,1)S(1)} %get-tuple-element.334, bf16[512,2,4,128]{0,3,2,1:T(8,128)(2,1)} %bitcast.124), kind=kOutput, calls=%fused_computation.25.clone.1 | convolution fusion | flops 543158272 | bytes 9978368 | tf_op jit(solution)/shard_map/while/body/eval_jaxpr/qgjd,ngd->qgjn/dot_general | solution.py:20
  370.8 4.9 %bitcast_add_fusion.5 = f32[128,4,8,128]{0,3,2,1:T(8,128)} fusion(f32[128,4,8,128]{0,3,2,1:T(8,128)} %get-tuple-element.322, f32[4,512,128,8]{2,1,3,0:T(8,128)S(1)} %copy-done.1, f32[128,4,8]{0,2,1:T(8,128)S(1)} %select_maximum_fusion.2, pred[512]{0:T(512)(128)(4,1)S(1)} %bitcast_reduce_fusion.2, f32[128,4,8]{0,2,1:T(8,128)S(1)} %get-tuple-element.309, ...), kind=kOutput, calls=%fused_computation.35.clone.1 | convolution fusion | flops 546832384 | bytes 13140481 | tf_op jit(solution)/shard_map/while/body/eval_jaxpr/qgjn,ngd->qgjd/dot_general | solution.py:29
  380.3 6.2 %fusion.69 = (f32[128,4,8]{0,2,1:T(8,128)S(1)}, f32[4,512,128,8]{2,1,3,0:T(8,128)}) fusion(pred[512]{0:T(512)(128)(4,1)S(1)} %bitcast_reduce_fusion.2, bf16[128,4,8,128]{3,0,2,1:T(8,128)(2,1)S(1)} %get-tuple-element.334, bf16[512,2,4,128]{0,3,2,1:T(8,128)(2,1)} %bitcast.124), kind=kOutput, calls=%fused_computation.25.clone.1 | convolution fusion | flops 543158272 | bytes 9978368 | tf_op jit(solution)/shard_map/while/body/eval_jaxpr/qgjd,ngd->qgjn/dot_general | solution.py:20
  386.6 4.6 %fusion.70 = f32[128,4,8]{0,2,1:T(8,128)S(1)} fusion(f32[4,512,128,8]{2,1,3,0:T(8,128)} %get-tuple-element.307, f32[128,4,8]{0,2,1:T(8,128)S(1)} %select_maximum_fusion.2, pred[512]{0:T(512)(128)(4,1)S(1)} %bitcast_reduce_fusion.2), kind=kLoop, calls=%fused_computation.29.clone.1 | loop fusion | flops 8384512 | bytes 8421888 | tf_op jit(solution)/shard_map/while/body/eval_jaxpr/reduce_sum | solution.py:28
  392.4 4.9 %bitcast_add_fusion.5 = f32[128,4,8,128]{0,3,2,1:T(8,128)} fusion(f32[128,4,8,128]{0,3,2,1:T(8,128)} %get-tuple-element.322, f32[4,512,128,8]{2,1,3,0:T(8,128)S(1)} %copy-done.1, f32[128,4,8]{0,2,1:T(8,128)S(1)} %select_maximum_fusion.2, pred[512]{0:T(512)(128)(4,1)S(1)} %bitcast_reduce_fusion.2, f32[128,4,8]{0,2,1:T(8,128)S(1)} %get-tuple-element.309, ...), kind=kOutput, calls=%fused_computation.35.clone.1 | convolution fusion | flops 546832384 | bytes 13140481 | tf_op jit(solution)/shard_map/while/body/eval_jaxpr/qgjn,ngd->qgjd/dot_general | solution.py:29
  397.3 25.3 %while.29 = (s32[]{:T(128)}, f32[128,4,8]{0,2,1:T(8,128)S(1)}, f32[128,4,8]{0,2,1:T(8,128)S(1)}, f32[128,4,8,128]{0,3,2,1:T(8,128)}, pred[2,128,512]{1,2,0:T(8,1...) while((s32[]{:T(128)}, f32[128,4,8]{0,2,1:T(8,128)S(1)}, ...), condition=%wide.region_13.14_spmd, body=%wide.region_10.13_spmd.sunk | while | flops 1097867264 | bytes 57213104 | solution.py:49
  (138 shorter events, 109.8 us)
Async XLA Ops:
  6.5 23.4 %copy-start = (bf16[16,64,1024]{2,1,0:T(8,128)(2,1)S(1)}, bf16[16,64,1024]{2,1,0:T(8,128)(2,1)}, u32[]{:S(2)}) copy-start(bf16[16,64,1024]{2,1,0:T(8,128)(2,1)} %param.12) | copy-start | bytes 6291460
  35.4 7.3 %copy-start.5 = (bf16[128,4096]{1,0:T(8,128)(2,1)S(1)}, bf16[128,4096]{1,0:T(8,128)(2,1)}, u32[]{:S(2)}) copy-start(bf16[128,4096]{1,0:T(8,128)(2,1)} %param.10) | copy-start | bytes 3145732
  35.4 189.8 %all-to-all-start.1 = ((bf16[32,2,64,1024]{3,2,1,0:T(8,128)(2,1)}), bf16[32,2,64,1024]{3,2,1,0:T(8,128)(2,1)}, u32[]{:S(2)}, u32[]{:S(2)}) async-start(bf16[32,2,64,1024]{3,2,1,0:T(8,128)(2,1)} %bitcast.128), calls=%async_computation.1 | async-start | bytes 16777216 | tf_op jit(solution)/shard_map/all_to_all | solution.py:77
  40.5 356.9 %all-gather.2.cloned.1.call-start = ((), (), s32[]{:S(2)}) async-start(), calls=%async_computation.2 | async-start | bytes 2359296 | tf_op jit(solution)/shard_map/all_gather | solution.py:101
  236.0 5.8 %copy-start.1 = (f32[4,512,128,8]{2,1,3,0:T(8,128)S(1)}, f32[4,512,128,8]{2,1,3,0:T(8,128)}, u32[]{:S(2)}) copy-start(f32[4,512,128,8]{2,1,3,0:T(8,128)} %get-tuple-element.307) | copy-start | bytes 25165828 | tf_op jit(solution)/shard_map/while
  256.9 5.8 %copy-start.1 = (f32[4,512,128,8]{2,1,3,0:T(8,128)S(1)}, f32[4,512,128,8]{2,1,3,0:T(8,128)}, u32[]{:S(2)}) copy-start(f32[4,512,128,8]{2,1,3,0:T(8,128)} %get-tuple-element.307) | copy-start | bytes 25165828 | tf_op jit(solution)/shard_map/while
  278.5 5.8 %copy-start.1 = (f32[4,512,128,8]{2,1,3,0:T(8,128)S(1)}, f32[4,512,128,8]{2,1,3,0:T(8,128)}, u32[]{:S(2)}) copy-start(f32[4,512,128,8]{2,1,3,0:T(8,128)} %get-tuple-element.307) | copy-start | bytes 25165828 | tf_op jit(solution)/shard_map/while
  300.1 5.8 %copy-start.1 = (f32[4,512,128,8]{2,1,3,0:T(8,128)S(1)}, f32[4,512,128,8]{2,1,3,0:T(8,128)}, u32[]{:S(2)}) copy-start(f32[4,512,128,8]{2,1,3,0:T(8,128)} %get-tuple-element.307) | copy-start | bytes 25165828 | tf_op jit(solution)/shard_map/while
  321.7 5.8 %copy-start.1 = (f32[4,512,128,8]{2,1,3,0:T(8,128)S(1)}, f32[4,512,128,8]{2,1,3,0:T(8,128)}, u32[]{:S(2)}) copy-start(f32[4,512,128,8]{2,1,3,0:T(8,128)} %get-tuple-element.307) | copy-start | bytes 25165828 | tf_op jit(solution)/shard_map/while
  343.3 5.8 %copy-start.1 = (f32[4,512,128,8]{2,1,3,0:T(8,128)S(1)}, f32[4,512,128,8]{2,1,3,0:T(8,128)}, u32[]{:S(2)}) copy-start(f32[4,512,128,8]{2,1,3,0:T(8,128)} %get-tuple-element.307) | copy-start | bytes 25165828 | tf_op jit(solution)/shard_map/while
  364.9 5.8 %copy-start.1 = (f32[4,512,128,8]{2,1,3,0:T(8,128)S(1)}, f32[4,512,128,8]{2,1,3,0:T(8,128)}, u32[]{:S(2)}) copy-start(f32[4,512,128,8]{2,1,3,0:T(8,128)} %get-tuple-element.307) | copy-start | bytes 25165828 | tf_op jit(solution)/shard_map/while
  386.6 5.8 %copy-start.1 = (f32[4,512,128,8]{2,1,3,0:T(8,128)S(1)}, f32[4,512,128,8]{2,1,3,0:T(8,128)}, u32[]{:S(2)}) copy-start(f32[4,512,128,8]{2,1,3,0:T(8,128)} %get-tuple-element.307) | copy-start | bytes 25165828 | tf_op jit(solution)/shard_map/while
  401.9 4.5 %copy-start.2 = (bf16[1,512,1024]{1,2,0:T(8,128)(2,1)S(1)}, bf16[1,512,1024]{1,2,0:T(8,128)(2,1)}, u32[]{:S(2)}) copy-start(bf16[1,512,1024]{1,2,0:T(8,128)(2,1)} %copy.79) | copy-start | bytes 3145732 | tf_op jit(solution)/shard_map/while
  401.9 4.5 %copy-start.3 = (f32[128,4,8,128]{0,3,2,1:T(8,128)S(1)}, f32[128,4,8,128]{0,3,2,1:T(8,128)}, u32[]{:S(2)}) copy-start(f32[128,4,8,128]{0,3,2,1:T(8,128)} %get-tuple-element.348) | copy-start | bytes 6291460 | tf_op jit(solution)/shard_map/while
  408.7 1.3 copy-start.4
  414.6 4.5 %copy-start.2 = (bf16[1,512,1024]{1,2,0:T(8,128)(2,1)S(1)}, bf16[1,512,1024]{1,2,0:T(8,128)(2,1)}, u32[]{:S(2)}) copy-start(bf16[1,512,1024]{1,2,0:T(8,128)(2,1)} %copy.79) | copy-start | bytes 3145732 | tf_op jit(solution)/shard_map/while
  414.6 4.5 %copy-start.3 = (f32[128,4,8,128]{0,3,2,1:T(8,128)S(1)}, f32[128,4,8,128]{0,3,2,1:T(8,128)}, u32[]{:S(2)}) copy-start(f32[128,4,8,128]{0,3,2,1:T(8,128)} %get-tuple-element.348) | copy-start | bytes 6291460 | tf_op jit(solution)/shard_map/while
  421.3 1.3 copy-start.4
Sparse Core Ops, SparseCore 0:
  43.2 30.7 all-gather.1
where the time goes:
time: 436 us; the launch traced here: 433 us
  waiting for transfers between devices  180 us (41%)
  matrix products  98.6 us (23%)
  local copies, waits for them, and re-layouts  68.7 us (16%)
  other arithmetic  45.5 us (10%)
  blocking collectives  20.5 us (5%)
  between operations  14.2 us (3%)
  starting transfers between devices  5.13 us (1%)
    all_to_all x1, waiting for transfers between devices, per_device(): lax.all_to_all(pages, 'pool', split_axis=0, concat_axis=0, tiled=True)  179 us
    dot_general x10, matrix products, attend_block(): jnp.einsum('qgjd,ngd->qgjn', queries_four, pairs[:, 0], preferred_element...  55.2 us
    dynamic_slice x28, local copies, waits for them, and re-layouts, attend_rows(): state, unused = lax.scan(advance, state, (pair_blocks, usable_blocks))  45.8 us
    dot_general x10, matrix products, attend_block(): jnp.einsum('qgjn,ngd->qgjd', weights.astype(jnp.bfloat16), pairs[:, 1], p...  43.4 us
    reduce_sum x10, other arithmetic, attend_block(): denom_sum = denom_sum * factor + jnp.sum(weights, axis=-1)  40.3 us
    all_to_all x1, blocking collectives, per_device(): lax.all_to_all(slot_page, 'pool', split_axis=0, concat_axis=0, tiled=True)  20.5 us
    while x38, local copies, waits for them, and re-layouts  12.3 us
  transfers between devices with their start and end apart: 2, of which 1 were waited for; matrix products, arithmetic and copies ran while one was open for 38% of the time, Pallas kernels for 0%

commit v1 on v0

v1 whole, which is shorter than its diff:
```python
import functools
import math

import jax
import jax.numpy as jnp
from jax import lax
from jax.experimental import pallas as pl
from jax.experimental.pallas import tpu as pltpu
from jax.sharding import PartitionSpec as P

KVH = 4
DH = 128
PAGE = 64
QB = 128
PAGES_DEV = 16
PAGES_REQ = 32
NY = 4
NZ = 8
NX = 4
CH = 4
CR = PAGE // CH
CK = PAGES_REQ * CR
SURE = 1280 // PAGE
RB = 256
ROWS = 1024
KC = 1024
BF = jnp.bfloat16
F32 = jnp.float32
MESH = pl.DeviceIdType.MESH
SCALE = math.log2(math.e) / math.sqrt(DH)
PLACE_OF = {0: 0, 1: 1, 7: 2, 2: 3, 6: 4, 3: 5, 5: 6, 4: 7}
GROUPS = {0: (0,), 1: (1, 7), 2: (2, 6), 3: (3, 5), 4: (4,)}


def dot(a, b, ca, cb):
    return lax.dot_general(a, b, (((ca,), (cb,)), ((), ())), preferred_element_type=F32)


def kernel(own_s, ids_s, len_s, own_v, q_hbm, span_hbm, store_hbm, out_ref, *scr):
    scr = list(scr)

    def take(n):
        got = scr[:n]
        del scr[:n]
        return got

    zb = [take(NZ) for _ in range(CH)]
    ysend = take(CH)
    rbuf = take(CH)
    (kvall, am, qraw, q2, acc, top, ltab, tab) = take(8)
    (loc_sem, tab_sem, list_ss, list_rs, z_ss, z_rs, y_ss, y_rs, x_ss, x_rs, p_ss, p_rs,
     sp_ss, sp_rs, spp_ss, spp_rs) = take(16)

    pool = lax.axis_index("pool")
    blk = lax.axis_index("blk")
    y, z = pool // NZ, pool % NZ
    x, c = blk // 2, blk % 2
    zr = (y * NZ + (z + 1) % NZ, blk)
    zl = (y * NZ + (z + NZ - 1) % NZ, blk)
    ydev = [(((y + d) % NY) * NZ + z, blk) for d in range(NY)]
    xdev = [(pool, ((x + d) % NX) * 2 + c) for d in range(NX)]
    mate = (pool, x * 2 + 1 - c)

    def rcopy(src, dst, ss, rs, dev):
        return pltpu.make_async_remote_copy(
            src_ref=src, dst_ref=dst, send_sem=ss, recv_sem=rs, device_id=dev, device_id_type=MESH)

    col = pl.multiple_of(c * (KVH * DH) + x * DH, DH)
    loads = []
    for h in range(CH):
        loads.append(pltpu.make_async_copy(
            store_hbm.at[:, pl.ds(h * CR, CR), pl.ds(col, DH)], zb[h][0], loc_sem.at[h]))
    for t in range(2):
        for g in range(KVH):
            loads.append(pltpu.make_async_copy(
                span_hbm.at[:, pl.ds((t * KVH + g) * DH, DH)], kvall.at[0, g, t, pl.ds(0, QB), :],
                loc_sem.at[4 + t * KVH + g]))
    loads.append(pltpu.make_async_copy(q_hbm, qraw, loc_sem.at[12]))
    for cp in loads:
        cp.start()
    barrier = pltpu.get_barrier_semaphore()
    near = [zr, zl] + ydev[1:] + xdev[1:] + [mate]
    for dev in near:
        pl.semaphore_signal(barrier, inc=1, device_id=dev, device_id_type=MESH)

    lane = lax.broadcasted_iota(jnp.int32, (8, 128), 1)
    row8 = lax.broadcasted_iota(jnp.int32, (8, 128), 0)
    owners_v = jnp.broadcast_to(own_v[...], (8, 128))
    seen = jnp.zeros((8, 128), jnp.int32)
    rank = jnp.zeros((8, 128), jnp.int32)
    page0 = jnp.zeros((8, 128), jnp.int32)
    page1 = jnp.zeros((8, 128), jnp.int32)
    for s in range(PAGES_REQ):
        o, ident = own_s[0, s], ids_s[0, s]
        hit = lane == o
        page0 = jnp.where(hit & (seen == 0), ident, page0)
        page1 = jnp.where(hit & (seen == 1), ident, page1)
        seen = seen + hit.astype(jnp.int32)
        rank = rank + ((owners_v == o) & (lane > s)).astype(jnp.int32)
    dd = ((owners_v >> 3) - y + NY) & (NY - 1)
    kk = (z - (owners_v & 7) + NZ) & (NZ - 1)
    jj = jnp.where(kk == 0, 0, jnp.where(kk < 4, 2 * kk - 1, jnp.where(kk == 4, 7, 2 * (8 - kk))))
    where_v = (dd * NZ + jj) * 2 + jnp.minimum(rank, 1)
    ltab[0] = jnp.where(row8 == 0, page0, jnp.where(row8 == 1, page1, where_v))

    limit = len_s[0]
    rowk = lax.broadcasted_iota(jnp.int32, (KC, DH), 0)
    am[0] = jnp.where(rowk // QB <= blk, 1.0, 0.0).astype(BF)
    for grp in range(2):
        within = rowk % CK
        pos = (within // CR) * PAGE + (grp * 2 + rowk // CK) * CR + within % CR
        am[1 + grp] = jnp.where(pos < limit, 1.0, 0.0).astype(BF)

    @pl.loop(0, KVH)
    def _(g):
        acc[g] = jnp.zeros((ROWS, 2 * DH), F32)
        top[g] = jnp.full((ROWS, DH), -1e30, F32)

    loads[12].wait()
    for hd in range(KVH * 8):
        qs = qraw[:, hd * DH:(hd + 1) * DH].astype(F32) * SCALE
        hi = qs.astype(BF)
        rows = pl.ds((hd % 8) * QB, QB)
        q2[hd // 8, rows, 0:DH] = hi
        q2[hd // 8, rows, DH:2 * DH] = (qs - hi.astype(F32)).astype(BF)
    for cp in loads[:12]:
        cp.wait()

    for j in range(1, 8):
        @pl.when(j > blk)
        def _():
            for g in range(KVH):
                first = kvall[0, g, 0, 0:1, :]
                kvall[0, g, 0, pl.ds(j * QB, QB), :] = jnp.broadcast_to(first, (QB, DH))
                kvall[0, g, 1, pl.ds(j * QB, QB), :] = jnp.zeros((QB, DH), BF)

    pl.semaphore_wait(barrier, len(near))

    def span_part(j):
        return kvall.at[0, :, :, pl.ds(pl.multiple_of(j * QB, QB), QB), :]

    def span_send(i):
        return rcopy(span_part(0), span_part(2 * i), sp_ss.at[i], sp_rs.at[i], xdev[i])

    def span_mate(i):
        return rcopy(span_part(2 * i), span_part(2 * i + 1 - 2 * c), spp_ss.at[i], spp_rs.at[i], mate)

    def span_start():
        for i in (1, 2, 3):
            @pl.when(x + i < NX)
            def _():
                span_send(i).start()

        @pl.when(c == 0)
        def _():
            span_mate(0).start()

    def span_pass(i):
        @pl.when(x >= i)
        def _():
            span_send(i).wait_recv()
            span_mate(i).start()

    def span_done():
        @pl.when(c == 1)
        def _():
            rcopy(span_part(0), span_part(1), spp_ss.at[0], spp_rs.at[0], mate).wait_recv()
        for i in (1, 2, 3):
            @pl.when(x >= i)
            def _():
                rcopy(span_part(2 * i), span_part(2 * i - 1 + 2 * c), spp_ss.at[i], spp_rs.at[i], mate).wait_recv()

    def list_send(d):
        return rcopy(ltab.at[0], ltab.at[d], list_ss.at[d], list_rs.at[d], ydev[d])

    HALF = PAGES_DEV // 2
    LO, HI = pl.ds(0, HALF), pl.ds(HALF, HALF)

    def z_up(h, k):
        if k < 3:
            return rcopy(zb[h][k], zb[h][k + 1], z_ss.at[h], z_rs.at[h, k + 1], zr)
        return rcopy(zb[h][3].at[LO], zb[h][4].at[LO], z_ss.at[h], z_rs.at[h, 4], zr)

    def z_down(h, k):
        src = (NZ - k) % NZ
        if k < 3:
            return rcopy(zb[h][src], zb[h][NZ - k - 1], z_ss.at[h], z_rs.at[h, NZ - k - 1], zl)
        return rcopy(zb[h][5].at[HI], zb[h][4].at[HI], z_ss.at[h], z_rs.at[h, 0], zl)

    def y_send(h, e, d):
        lo = 0 if e == 0 else 2 * (2 * e - 1)
        part = pl.ds(lo, 2 * len(GROUPS[e]))
        return rcopy(ysend[h].at[d, part], rbuf[h].at[d, part], y_ss.at[h], y_rs.at[h], ydev[(NY - d) % NY])

    def pack(h, e):
        for k in GROUPS[e]:
            j = PLACE_OF[k]
            owner = y * NZ + (z + NZ - k) % NZ
            for d in range(NY):
                for slot in range(2):
                    page = tab[d, slot, owner]
                    dst = rbuf[h].at[0] if d == 0 else ysend[h].at[d]
                    dst[2 * j + slot] = zb[h][k][page]
        for d in range(1, NY):
            y_send(h, e, d).start()

    def own(h):
        z_up(h, 0).start()
        z_down(h, 0).start()

    def ring(h, k):
        z_up(h, k - 1).wait_recv()
        if k < 4:
            z_up(h, k).start()
        z_down(h, k - 1).wait_recv()
        if k < 4:
            z_down(h, k).start()
        pack(h, k)

    def part(h, r):
        g = (x + NX - r) % NX
        return lambda t, half=None: kvall.at[
            1 + h // 2, g, t,
            pl.ds((h % 2) * CK + (0 if half is None else half * (CK // 2)), CK if half is None else CK // 2), :]

    def x_send(h, up):
        mine = part(h, 0)(c)
        return rcopy(mine, mine, x_ss.at[h], x_rs.at[h, 0 if up else 1], xdev[1] if up else xdev[3])

    def x_recv(h, up):
        got = part(h, 1 if up else 3)(c)
        return rcopy(got, got, x_ss.at[h], x_rs.at[h, 0 if up else 1], xdev[1])

    def x_pass(h, up):
        got = part(h, 1 if up else 3)(c, 0 if up else 1)
        return rcopy(got, got, x_ss.at[h], x_rs.at[h, 2 if up else 3], xdev[1] if up else xdev[3])

    def x_far(h, up):
        got = part(h, 2)(c, 0 if up else 1)
        return rcopy(got, got, x_ss.at[h], x_rs.at[h, 2 if up else 3], xdev[1])

    def m_send(h, r):
        mine = part(h, r)(c)
        return rcopy(mine, mine, p_ss.at[h], p_rs.at[h, r], mate)

    def m_recv(h, r):
        got = part(h, r)(1 - c)
        return rcopy(got, got, p_ss.at[h], p_rs.at[h, r], mate)

    def compact(h):
        whole = rbuf[h].at[pl.ds(1, NY - 1)]
        rcopy(whole, whole, y_ss.at[h], y_rs.at[h], mate).wait_recv()
        grp, base = 1 + h // 2, (h % 2) * CK
        rows = lax.broadcasted_iota(jnp.int32, (CR, DH), 0)
        fill = None
        for s in range(PAGES_REQ):
            at = tab[0, 2, s]
            page = rbuf[h][at // 16, at % 16]
            if s == 0:
                fill = jnp.broadcast_to(page[0:1].astype(F32), (CR, DH)) * (1 - c).astype(F32)
            if s >= SURE:
                page = jnp.where(rows < limit - (s * PAGE + h * CR), page.astype(F32), fill).astype(BF)
            kvall[grp, x, c, pl.ds(base + s * CR, CR), :] = page
        x_send(h, True).start()
        x_send(h, False).start()
        m_send(h, 0).start()

    def neighbours(h):
        x_recv(h, True).wait_recv()
        x_pass(h, True).start()
        x_recv(h, False).wait_recv()
        x_pass(h, False).start()
        m_send(h, 1).start()
        m_send(h, 3).start()

    def opposite(h):
        x_far(h, True).wait_recv()
        x_far(h, False).wait_recv()
        m_send(h, 2).start()

    for i in (1, 2, 3):
        list_send(i).start()
    own(0)
    span_start()
    own(1)
    for i in (1, 2, 3):
        list_send(i).wait_recv()
    cp = pltpu.make_async_copy(ltab, tab, tab_sem.at[0])
    cp.start()
    cp.wait()
    for h in range(CH):
        pack(h, 0)

    def E(h, k): return lambda: ring(h, k)
    def O(h): return lambda: own(h)
    def C(h): return lambda: compact(h)
    def N(h): return lambda: neighbours(h)
    def F(h): return lambda: opposite(h)
    def SP(i): return lambda: span_pass(i)

    plan = PLAN(E, O, C, N, F, SP, span_done)
    for step in plan[-1]:
        step()

    @pl.loop(0, 12)
    def _(u):
        grp = u // 4
        i = u % 4
        r = i + i // 2 - 2 * (i // 3)
        g = (x + NX - r) % NX

        def hook(place):
            for at, steps in plan.items():
                if at >= 0 and at % 4 == place:
                    @pl.when(u == at // 4)
                    def _():
                        for step in steps:
                            step()

        hook(0)
        for uu in range(4, 12):
            @pl.when(u == uu)
            def _():
                rr = (0, 1, 3, 2)[uu % 4]
                for h in (0, 1):
                    m_recv((uu // 4 - 1) * 2 + h, rr).wait_recv()
        keys = kvall[grp, g, 0]
        vals = kvall[grp, g, 1]
        k2 = jnp.concatenate([keys, keys], axis=1)
        v2 = jnp.concatenate([vals, am[grp]], axis=1)
        token = lax.broadcasted_iota(jnp.int32, (RB, QB), 0) % QB
        key = lax.broadcasted_iota(jnp.int32, (RB, QB), 1)
        inside = (key <= token) | (grp > 0)

        def scores(rb):
            s = dot(q2[g, pl.ds(rb * RB, RB), :], k2, 1, 1)
            return jnp.concatenate([jnp.where(inside, s[:, :QB], -1e30), s[:, QB:]], axis=1)

        def granule(rb, s):
            rows = pl.ds(rb * RB, RB)
            old = top[g, rows, 0:1]
            new = jnp.maximum(old, jnp.max(s, axis=1, keepdims=True))
            p = jnp.exp2(s - new).astype(BF)
            acc[g, rows, :] = acc[g, rows, :] * jnp.exp2(old - new) + dot(p, v2, 1, 0)
            top[g, rows, :] = jnp.broadcast_to(new, (RB, DH))

        n = ROWS // RB
        for pair in range(n // 2):
            if pair:
                hook(pair * 2)
            s0 = scores(2 * pair)
            s1 = scores(2 * pair + 1)
            granule(2 * pair, s0)
            granule(2 * pair + 1, s1)

        @pl.when(grp == 2)
        def _():
            for hd in range(8):
                a = acc[g, pl.ds(hd * QB, QB), :]
                out_ref[:, pl.ds(pl.multiple_of((g * 8 + hd) * DH, DH), DH)] = (
                    a[:, :DH] / a[:, DH:]).astype(BF)

    for i in (1, 2, 3):
        list_send(i).wait_send()

        @pl.when(x + i < NX)
        def _():
            span_send(i).wait_send()

        @pl.when(x >= i)
        def _():
            span_mate(i).wait_send()

    @pl.when(c == 0)
    def _():
        span_mate(0).wait_send()
    for h in range(CH):
        for ref, ss in (
            (kvall.at[1, pl.ds(0, 3), 0, pl.ds(0, CK), :], x_ss.at[h]),
            (kvall.at[1, :, 0, pl.ds(0, CK), :], p_ss.at[h]),
            (ysend[h].at[pl.ds(1, NY - 1)], y_ss.at[h]),
        ):
            rcopy(ref, ref, ss, ss, mate).wait_send()
        z_wait = kvall.at[1, 0, :, pl.ds(0, 7 * PAGES_DEV * CR // 2), :]
        rcopy(z_wait, z_wait, z_ss.at[h], z_ss.at[h], mate).wait_send()


def PLAN(E, O, C, N, F, SP, SD):
    return {
        -1: [E(0, 1), E(0, 2), E(1, 1), E(0, 3), O(2), E(1, 2), SP(1), E(0, 4), E(1, 3), C(0), SP(3), E(2, 1), SP(2), SD],
        0: [E(1, 4), O(3), E(2, 2)],
        2: [C(1), E(3, 1), E(2, 3)],
        4: [N(0)],
        6: [E(3, 2), E(2, 4)],
        8: [C(2), E(3, 3), F(0)],
        10: [N(1)],
        14: [E(3, 4), F(1)],
        16: [C(3)],
        18: [N(2)],
        22: [F(2)],
        28: [N(3)],
        36: [F(3)],
    }


def per_device(queries, span_kv, kv_store, page_ids, page_owner, prefix_len):
    anyw = pl.BlockSpec(memory_space=pl.ANY)
    smem = pl.BlockSpec(memory_space=pltpu.SMEM)
    vmem = pl.BlockSpec(memory_space=pltpu.VMEM)
    dma = pltpu.SemaphoreType.DMA
    owners_row = jnp.pad(page_owner, ((0, 0), (0, 128 - PAGES_REQ)))
    scratch = [pltpu.VMEM((PAGES_DEV, CR, DH), BF) for _ in range(CH * NZ)]
    scratch += [pltpu.VMEM((NY, 2 * NZ, CR, DH), BF) for _ in range(2 * CH)]
    scratch += [
        pltpu.VMEM((3, KVH, 2, KC, DH), BF),
        pltpu.VMEM((3, KC, DH), BF),
        pltpu.VMEM((QB, KVH * 8 * DH), BF),
        pltpu.VMEM((KVH, ROWS, 2 * DH), BF),
        pltpu.VMEM((KVH, ROWS, 2 * DH), F32),
        pltpu.VMEM((KVH, ROWS, DH), F32),
        pltpu.VMEM((NY, 8, 128), jnp.int32),
        pltpu.SMEM((NY, 8, 128), jnp.int32),
        dma((13,)), dma((1,)), dma((4,)), dma((4,)),
        dma((CH,)), dma((CH, NZ)),
        dma((CH,)), dma((CH,)),
        dma((CH,)), dma((CH, 4)),
        dma((CH,)), dma((CH, 4)),
        dma((4,)), dma((4,)), dma((4,)), dma((4,)),
    ]
    return pl.pallas_call(
        kernel,
        out_shape=jax.ShapeDtypeStruct(queries.shape, BF),
        in_specs=[smem, smem, smem, vmem, anyw, anyw, anyw],
        out_specs=vmem,
        scratch_shapes=scratch,
        compiler_params=pltpu.CompilerParams(
            vmem_limit_bytes=56 * 2**20, collective_id=0, has_side_effects=True),
        cost_estimate=pl.CostEstimate(
            flops=4 * 4096 * 3072 * 128, bytes_accessed=4 * 2**20, transcendentals=4096 * 3072),
    )(page_owner, page_ids, prefix_len, owners_row, queries, span_kv, kv_store)


def solution(mesh):
    in_specs = (
        P(("pool", "blk"), None),
        P(("pool", "blk"), None),
        P("pool", None, None),
        P("pool", None),
        P("pool", None),
        P("pool"),
    )
    return jax.shard_map(
        per_device, mesh=mesh, in_specs=in_specs, out_specs=P(("pool", "blk"), None), check_vma=False
    )
```

time: 436 us -> 77.6 us (0.18)
  the two profiles are of different devices: /device:TPU:1 before, /device:TPU:2 now
where the time goes in v1:
time: 77.6 us; the launch traced here: 77.5 us
  Pallas kernels  73.4 us (95%)
  local copies, waits for them, and re-layouts  3.46 us (4%)
    pallas_call x1, Pallas kernels, per_device(): pl.pallas_call(kernel, out_shape=jax.ShapeDtypeStruct(queries.shape, BF),...  73.4 us
    unnamed x1, local copies, waits for them, and re-layouts  2.29 us

profile of v1, /device:TPU:2, one launch (start us, length us, event | category | flops | bytes accessed | tf_op | source)
XLA Modules:
  0.0 77.5 jit_solution(3242826256635256632)
XLA Ops:
  0.7 1.2 %pad.4.own_v = s32[1,128]{1,0:T(1,128)} pad(s32[1,32]{1,0:T(1,128)} %own_s.1, s32[]{:T(128)} %constant.0.clone.1), padding=0_0x0_96 | pad | bytes 644 | tf_op jit(solution)/shard_map/jit(_pad)/pad | solution.py:411
  1.8 73.4 %shard_map.64 = bf16[128,4096]{1,0:T(8,128)(2,1)} custom-call(s32[1,32]{1,0:T(1,128)} %own_s.1, s32[1,32]{1,0:T(1,128)} %ids_s.1, s32[1]{0:T(128)S(6)} %copy.8.len_s, s32[1,128]{1,0:T(1,128)} %pad.4.own_v, bf16[128,4096]{1,0:T(8,128)(2,1)} %q_hbm.1, bf16[128,1024]{1,0:T(8,128)(2,1)} %span_hbm.1, bf16[16,64,1024]{2,1,0:T(8,128)(2,1)} %store_hbm.1), custom_call_target="tpu_custom_call" | custom-call | flops 6442450944 | bytes 4194304 | tf_op jit(solution)/shard_map/pallas_call | solution.py:430
  75.2 2.3 %copy.9 = bf16[128,4096]{1,0:T(8,128)(2,1)} copy(bf16[128,4096]{1,0:T(8,128)(2,1)} %shard_map.64) | data formatting | bytes 2097152

commit v2 on v1

--- a/solution.py
+++ b/solution.py
@@ -29,7 +29,12 @@
 MESH = pl.DeviceIdType.MESH
 SCALE = math.log2(math.e) / math.sqrt(DH)
 PLACE_OF = {0: 0, 1: 1, 7: 2, 2: 3, 6: 4, 3: 5, 5: 6, 4: 7}
-GROUPS = {0: (0,), 1: (1, 7), 2: (2, 6), 3: (3, 5), 4: (4,)}
+GROUPS = {0: (0,), 1: (1, 7), 2: (2, 6)}
+NEAR = 10
+FAR = 6
+COLS = (0, 1, -1, 2, -2)
+FAR_SLOTS = ((2, 1, 0), (2, 1, 1), (6, 2, 0), (6, 2, 1), (2, 3, 0), (6, 4, 1))
+FAR_RUNS = ((0, 2, 1), (2, 2, 2), (4, 1, 3), (5, 1, 4))
 
 
 def dot(a, b, ca, cb):
@@ -44,12 +49,13 @@
         del scr[:n]
         return got
 
-    zb = [take(NZ) for _ in range(CH)]
+    zb = [dict(zip((0, 1, 2, 6, 7), take(5))) for _ in range(CH)]
     ysend = take(CH)
+    fsend = take(CH)
     rbuf = take(CH)
-    (kvall, am, qraw, q2, acc, top, ltab, tab) = take(8)
-    (loc_sem, tab_sem, list_ss, list_rs, z_ss, z_rs, y_ss, y_rs, x_ss, x_rs, p_ss, p_rs,
-     sp_ss, sp_rs, spp_ss, spp_rs) = take(16)
+    (kvall, am, qraw, q2, acc, top, ltab, tab, wtab, wtab_s) = take(10)
+    (loc_sem, tab_sem, list_ss, list_rs, z_ss, z_rs, y_ss, y_rs, f_ss, f_rs, x_ss, x_rs, p_ss, p_rs,
+     sp_ss, sp_rs, spp_ss, spp_rs) = take(18)
 
     pool = lax.axis_index("pool")
     blk = lax.axis_index("blk")
@@ -79,17 +85,21 @@
     for cp in loads:
         cp.start()
     barrier = pltpu.get_barrier_semaphore()
-    near = [zr, zl] + ydev[1:] + xdev[1:] + [mate]
+    def at(dz, d):
+        return (((y + d) % NY) * NZ + (z + NZ + dz) % NZ, blk)
+
+    near = [at(dz, d) for dz in COLS for d in range(NY) if dz or d] + xdev[1:] + [mate]
     for dev in near:
         pl.semaphore_signal(barrier, inc=1, device_id=dev, device_id_type=MESH)
 
-    lane = lax.broadcasted_iota(jnp.int32, (8, 128), 1)
-    row8 = lax.broadcasted_iota(jnp.int32, (8, 128), 0)
-    owners_v = jnp.broadcast_to(own_v[...], (8, 128))
-    seen = jnp.zeros((8, 128), jnp.int32)
-    rank = jnp.zeros((8, 128), jnp.int32)
-    page0 = jnp.zeros((8, 128), jnp.int32)
-    page1 = jnp.zeros((8, 128), jnp.int32)
+    shape = (8, PAGES_REQ)
+    lane = lax.broadcasted_iota(jnp.int32, shape, 1)
+    row8 = lax.broadcasted_iota(jnp.int32, shape, 0)
+    owners_v = jnp.broadcast_to(own_v[...], shape)
+    seen = jnp.zeros(shape, jnp.int32)
+    rank = jnp.zeros(shape, jnp.int32)
+    page0 = jnp.zeros(shape, jnp.int32)
+    page1 = jnp.zeros(shape, jnp.int32)
     for s in range(PAGES_REQ):
         o, ident = own_s[0, s], ids_s[0, s]
         hit = lane == o
@@ -101,40 +111,44 @@
     kk = (z - (owners_v & 7) + NZ) & (NZ - 1)
     jj = jnp.where(kk == 0, 0, jnp.where(kk < 4, 2 * kk - 1, jnp.where(kk == 4, 7, 2 * (8 - kk))))
     where_v = (dd * NZ + jj) * 2 + jnp.minimum(rank, 1)
-    ltab[0] = jnp.where(row8 == 0, page0, jnp.where(row8 == 1, page1, where_v))
+    table = jnp.where(row8 == 0, page0 + PAGES_DEV * page1, where_v)
+    ltab[0, 0] = jnp.zeros((1, 128), jnp.int32)
+    ltab[0, 0, :, 0:PAGES_REQ] = table[0:1]
+    wtab[...] = jnp.zeros((1, 128), jnp.int32)
+    wtab[:, 0:PAGES_REQ] = table[1:2]
 
     limit = len_s[0]
-    rowk = lax.broadcasted_iota(jnp.int32, (KC, DH), 0)
-    am[0] = jnp.where(rowk // QB <= blk, 1.0, 0.0).astype(BF)
-    for grp in range(2):
-        within = rowk % CK
-        pos = (within // CR) * PAGE + (grp * 2 + rowk // CK) * CR + within % CR
-        am[1 + grp] = jnp.where(pos < limit, 1.0, 0.0).astype(BF)
-
-    @pl.loop(0, KVH)
-    def _(g):
-        acc[g] = jnp.zeros((ROWS, 2 * DH), F32)
-        top[g] = jnp.full((ROWS, DH), -1e30, F32)
-
-    loads[12].wait()
-    for hd in range(KVH * 8):
-        qs = qraw[:, hd * DH:(hd + 1) * DH].astype(F32) * SCALE
-        hi = qs.astype(BF)
-        rows = pl.ds((hd % 8) * QB, QB)
-        q2[hd // 8, rows, 0:DH] = hi
-        q2[hd // 8, rows, DH:2 * DH] = (qs - hi.astype(F32)).astype(BF)
     for cp in loads[:12]:
         cp.wait()
-
-    for j in range(1, 8):
-        @pl.when(j > blk)
-        def _():
-            for g in range(KVH):
-                first = kvall[0, g, 0, 0:1, :]
-                kvall[0, g, 0, pl.ds(j * QB, QB), :] = jnp.broadcast_to(first, (QB, DH))
-                kvall[0, g, 1, pl.ds(j * QB, QB), :] = jnp.zeros((QB, DH), BF)
-
     pl.semaphore_wait(barrier, len(near))
+
+    def prepare():
+        rowk = lax.broadcasted_iota(jnp.int32, (KC, DH), 0)
+        am[0] = jnp.where(rowk // QB <= blk, 1.0, 0.0).astype(BF)
+        for grp in range(2):
+            within = rowk % CK
+            pos = (within // CR) * PAGE + (grp * 2 + rowk // CK) * CR + within % CR
+            am[1 + grp] = jnp.where(pos < limit, 1.0, 0.0).astype(BF)
+
+        @pl.loop(0, KVH)
+        def _(g):
+            acc[g] = jnp.zeros((ROWS, 2 * DH), F32)
+            top[g] = jnp.full((ROWS, DH), -1e30, F32)
+
+        loads[12].wait()
+        for hd in range(KVH * 8):
+            qs = qraw[:, hd * DH:(hd + 1) * DH].astype(F32) * SCALE
+            hi = qs.astype(BF)
+            rows = pl.ds((hd % 8) * QB, QB)
+            q2[hd // 8, rows, 0:DH] = hi
+            q2[hd // 8, rows, DH:2 * DH] = (qs - hi.astype(F32)).astype(BF)
+        for j in range(1, 8):
+            @pl.when(j > blk)
+            def _():
+                for g in range(KVH):
+                    first = kvall[0, g, 0, 0:1, :]
+                    kvall[0, g, 0, pl.ds(j * QB, QB), :] = jnp.broadcast_to(first, (QB, DH))
+                    kvall[0, g, 1, pl.ds(j * QB, QB), :] = jnp.zeros((QB, DH), BF)
 
     def span_part(j):
         return kvall.at[0, :, :, pl.ds(pl.multiple_of(j * QB, QB), QB), :]
@@ -170,39 +184,74 @@
             def _():
                 rcopy(span_part(2 * i), span_part(2 * i - 1 + 2 * c), spp_ss.at[i], spp_rs.at[i], mate).wait_recv()
 
-    def list_send(d):
-        return rcopy(ltab.at[0], ltab.at[d], list_ss.at[d], list_rs.at[d], ydev[d])
-
-    HALF = PAGES_DEV // 2
-    LO, HI = pl.ds(0, HALF), pl.ds(HALF, HALF)
+    def list_send(col, d):
+        ss, rs = (list_ss.at[0], list_rs.at[0]) if col == 0 else (list_ss.at[1], list_rs.at[1])
+        return rcopy(ltab.at[0, 0], ltab.at[col, d], ss, rs, at(-COLS[col], d))
+
+    def lists_start():
+        for col in range(len(COLS)):
+            for d in range(NY):
+                if col or d:
+                    list_send(col, d).start()
+
+    def lists_wait(recv):
+        for i, part in ((0, ltab.at[0, pl.ds(1, NY - 1)]), (1, ltab.at[pl.ds(1, 4)])):
+            cp = rcopy(part, part, list_ss.at[i], list_rs.at[i], mate)
+            if recv:
+                cp.wait_recv()
+            else:
+                cp.wait_send()
+
+    def tables():
+        lists_wait(True)
+        cps = [pltpu.make_async_copy(ltab, tab, tab_sem.at[0]), pltpu.make_async_copy(wtab, wtab_s, tab_sem.at[1])]
+        for cp in cps:
+            cp.start()
+        for cp in cps:
+            cp.wait()
 
     def z_up(h, k):
-        if k < 3:
-            return rcopy(zb[h][k], zb[h][k + 1], z_ss.at[h], z_rs.at[h, k + 1], zr)
-        return rcopy(zb[h][3].at[LO], zb[h][4].at[LO], z_ss.at[h], z_rs.at[h, 4], zr)
+        return rcopy(zb[h][k], zb[h][k + 1], z_ss.at[h], z_rs.at[h, k + 1], zr)
 
     def z_down(h, k):
-        src = (NZ - k) % NZ
-        if k < 3:
-            return rcopy(zb[h][src], zb[h][NZ - k - 1], z_ss.at[h], z_rs.at[h, NZ - k - 1], zl)
-        return rcopy(zb[h][5].at[HI], zb[h][4].at[HI], z_ss.at[h], z_rs.at[h, 0], zl)
+        return rcopy(zb[h][(NZ - k) % NZ], zb[h][NZ - k - 1], z_ss.at[h], z_rs.at[h, NZ - k - 1], zl)
 
     def y_send(h, e, d):
         lo = 0 if e == 0 else 2 * (2 * e - 1)
         part = pl.ds(lo, 2 * len(GROUPS[e]))
-        return rcopy(ysend[h].at[d, part], rbuf[h].at[d, part], y_ss.at[h], y_rs.at[h], ydev[(NY - d) % NY])
+        return rcopy(ysend[h].at[d, part], rbuf[h].at[d, part], y_ss.at[h], y_rs.at[h], at(0, NY - d))
+
+    def f_send(h, lo, n, col, d):
+        return rcopy(fsend[h].at[d, pl.ds(lo, n)], rbuf[h].at[d, pl.ds(NEAR + lo, n)], f_ss.at[h], f_rs.at[h],
+                     at(COLS[col], NY - d))
 
     def pack(h, e):
+        pages = {}
         for k in GROUPS[e]:
-            j = PLACE_OF[k]
             owner = y * NZ + (z + NZ - k) % NZ
             for d in range(NY):
                 for slot in range(2):
-                    page = tab[d, slot, owner]
-                    dst = rbuf[h].at[0] if d == 0 else ysend[h].at[d]
-                    dst[2 * j + slot] = zb[h][k][page]
+                    both = tab[0, d, 0, owner]
+                    pages[k, d, slot] = both >> 4 if slot else both & 15
+        got = {key: zb[h][key[0]][page] for key, page in pages.items()}
+        for (k, d, slot), value in got.items():
+            dst = rbuf[h].at[0] if d == 0 else ysend[h].at[d]
+            dst[2 * PLACE_OF[k] + slot] = value
         for d in range(1, NY):
             y_send(h, e, d).start()
+
+    def pack_far(h):
+        pages = {}
+        for d in range(NY):
+            for i, (k, col, slot) in enumerate(FAR_SLOTS):
+                both = tab[col, d, 0, y * NZ + (z + NZ - k) % NZ]
+                pages[d, i] = both >> 4 if slot else both & 15
+        got = {key: zb[h][FAR_SLOTS[key[1]][0]][page] for key, page in pages.items()}
+        for (d, i), value in got.items():
+            fsend[h][d, i] = value
+        for lo, n, col in FAR_RUNS:
+            for d in range(NY):
+                f_send(h, lo, n, col, d).start()
 
     def own(h):
         z_up(h, 0).start()
@@ -210,12 +259,11 @@
 
     def ring(h, k):
         z_up(h, k - 1).wait_recv()
-        if k < 4:
-            z_up(h, k).start()
+        if k == 1:
+            z_up(h, 1).start()
         z_down(h, k - 1).wait_recv()
-        if k < 4:
-            z_down(h, k).start()
-        pack(h, k)
+        if k == 1:
+            z_down(h, 1).start()
 
     def part(h, r):
         g = (x + NX - r) % NX
@@ -248,14 +296,16 @@
         return rcopy(got, got, p_ss.at[h], p_rs.at[h, r], mate)
 
     def compact(h):
-        whole = rbuf[h].at[pl.ds(1, NY - 1)]
-        rcopy(whole, whole, y_ss.at[h], y_rs.at[h], mate).wait_recv()
+        part_in = rbuf[h].at[pl.ds(1, NY - 1), pl.ds(0, NEAR)]
+        rcopy(part_in, part_in, y_ss.at[h], y_rs.at[h], mate).wait_recv()
+        part_in = rbuf[h].at[:, pl.ds(NEAR, FAR)]
+        rcopy(part_in, part_in, f_ss.at[h], f_rs.at[h], mate).wait_recv()
         grp, base = 1 + h // 2, (h % 2) * CK
         rows = lax.broadcasted_iota(jnp.int32, (CR, DH), 0)
         fill = None
-        for s in range(PAGES_REQ):
-            at = tab[0, 2, s]
-            page = rbuf[h][at // 16, at % 16]
+        places = [wtab_s[0, s] for s in range(PAGES_REQ)]
+        pages = [rbuf[h][place >> 4, place & 15] for place in places]
+        for s, page in enumerate(pages):
             if s == 0:
                 fill = jnp.broadcast_to(page[0:1].astype(F32), (CR, DH)) * (1 - c).astype(F32)
             if s >= SURE:
@@ -278,27 +328,16 @@
         x_far(h, False).wait_recv()
         m_send(h, 2).start()
 
-    for i in (1, 2, 3):
-        list_send(i).start()
-    own(0)
-    span_start()
-    own(1)
-    for i in (1, 2, 3):
-        list_send(i).wait_recv()
-    cp = pltpu.make_async_copy(ltab, tab, tab_sem.at[0])
-    cp.start()
-    cp.wait()
-    for h in range(CH):
-        pack(h, 0)
-
-    def E(h, k): return lambda: ring(h, k)
+    def R(h, k): return lambda: ring(h, k)
+    def Q(h, e): return lambda: pack(h, e)
+    def Z(h): return lambda: pack_far(h)
     def O(h): return lambda: own(h)
     def C(h): return lambda: compact(h)
     def N(h): return lambda: neighbours(h)
     def F(h): return lambda: opposite(h)
     def SP(i): return lambda: span_pass(i)
 
-    plan = PLAN(E, O, C, N, F, SP, span_done)
+    plan = PLAN(R, Q, Z, O, C, N, F, SP, span_done, lists_start, span_start, tables, prepare)
     for step in plan[-1]:
         step()
 
@@ -360,9 +399,8 @@
                 out_ref[:, pl.ds(pl.multiple_of((g * 8 + hd) * DH, DH), DH)] = (
                     a[:, :DH] / a[:, DH:]).astype(BF)
 
+    lists_wait(False)
     for i in (1, 2, 3):
-        list_send(i).wait_send()
-
         @pl.when(x + i < NX)
         def _():
             span_send(i).wait_send()
@@ -379,27 +417,25 @@
             (kvall.at[1, pl.ds(0, 3), 0, pl.ds(0, CK), :], x_ss.at[h]),
             (kvall.at[1, :, 0, pl.ds(0, CK), :], p_ss.at[h]),
             (ysend[h].at[pl.ds(1, NY - 1)], y_ss.at[h]),
+            (fsend[h], f_ss.at[h]),
         ):
             rcopy(ref, ref, ss, ss, mate).wait_send()
-        z_wait = kvall.at[1, 0, :, pl.ds(0, 7 * PAGES_DEV * CR // 2), :]
+        z_wait = kvall.at[1, 0, 0, pl.ds(0, 4 * PAGES_DEV * CR), :]
         rcopy(z_wait, z_wait, z_ss.at[h], z_ss.at[h], mate).wait_send()
 
 
-def PLAN(E, O, C, N, F, SP, SD):
+def PLAN(R, Q, Z, O, C, N, F, SP, SD, LS, SS, LT, PR):
     return {
-        -1: [E(0, 1), E(0, 2), E(1, 1), E(0, 3), O(2), E(1, 2), SP(1), E(0, 4), E(1, 3), C(0), SP(3), E(2, 1), SP(2), SD],
-        0: [E(1, 4), O(3), E(2, 2)],
-        2: [C(1), E(3, 1), E(2, 3)],
-        4: [N(0)],
-        6: [E(3, 2), E(2, 4)],
-        8: [C(2), E(3, 3), F(0)],
-        10: [N(1)],
-        14: [E(3, 4), F(1)],
-        16: [C(3)],
-        18: [N(2)],
-        22: [F(2)],
-        28: [N(3)],
-        36: [F(3)],
+        -1: [O(0), LS, SS, O(1), PR, R(0, 1), LT, O(2), Q(0, 0), Q(0, 1), R(1, 1), O(3), R(0, 2), Q(0, 2), Z(0), Q(1, 0), Q(1, 1), R(2, 1), Q(2, 0), Q(2, 1), R(1, 2), Q(1, 2), Z(1), R(3, 1), Q(3, 0), Q(3, 1), SP(1), SP(3), SP(2), C(0), R(2, 2), Q(2, 2), Z(2), SD],
+        0: [R(3, 2), Q(3, 2), Z(3)],
+        4: [C(1)],
+        8: [N(0)],
+        12: [C(2)],
+        16: [N(1), F(0)],
+        20: [C(3)],
+        24: [N(2), F(1)],
+        30: [N(3), F(2)],
+        38: [F(3)],
     }
 
 
@@ -408,9 +444,10 @@
     smem = pl.BlockSpec(memory_space=pltpu.SMEM)
     vmem = pl.BlockSpec(memory_space=pltpu.VMEM)
     dma = pltpu.SemaphoreType.DMA
-    owners_row = jnp.pad(page_owner, ((0, 0), (0, 128 - PAGES_REQ)))
-    scratch = [pltpu.VMEM((PAGES_DEV, CR, DH), BF) for _ in range(CH * NZ)]
-    scratch += [pltpu.VMEM((NY, 2 * NZ, CR, DH), BF) for _ in range(2 * CH)]
+    scratch = [pltpu.VMEM((PAGES_DEV, CR, DH), BF) for _ in range(CH * 5)]
+    scratch += [pltpu.VMEM((NY, NEAR, CR, DH), BF) for _ in range(CH)]
+    scratch += [pltpu.VMEM((NY, FAR, CR, DH), BF) for _ in range(CH)]
+    scratch += [pltpu.VMEM((NY, NEAR + FAR, CR, DH), BF) for _ in range(CH)]
     scratch += [
         pltpu.VMEM((3, KVH, 2, KC, DH), BF),
         pltpu.VMEM((3, KC, DH), BF),
@@ -418,11 +455,13 @@
         pltpu.VMEM((KVH, ROWS, 2 * DH), BF),
         pltpu.VMEM((KVH, ROWS, 2 * DH), F32),
         pltpu.VMEM((KVH, ROWS, DH), F32),
-        pltpu.VMEM((NY, 8, 128), jnp.int32),
-        pltpu.SMEM((NY, 8, 128), jnp.int32),
-        dma((13,)), dma((1,)), dma((4,)), dma((4,)),
+        pltpu.VMEM((len(COLS), NY, 1, 128), jnp.int32),
+        pltpu.SMEM((len(COLS), NY, 1, 128), jnp.int32),
+        pltpu.VMEM((1, 128), jnp.int32),
+        pltpu.SMEM((1, 128), jnp.int32),
+        dma((13,)), dma((2,)), dma((2,)), dma((2,)),
         dma((CH,)), dma((CH, NZ)),
-        dma((CH,)), dma((CH,)),
+        dma((CH,)), dma((CH,)), dma((CH,)), dma((CH,)),
         dma((CH,)), dma((CH, 4)),
         dma((CH,)), dma((CH, 4)),
         dma((4,)), dma((4,)), dma((4,)), dma((4,)),
@@ -437,7 +476,7 @@
             vmem_limit_bytes=56 * 2**20, collective_id=0, has_side_effects=True),
         cost_estimate=pl.CostEstimate(
             flops=4 * 4096 * 3072 * 128, bytes_accessed=4 * 2**20, transcendentals=4096 * 3072),
-    )(page_owner, page_ids, prefix_len, owners_row, queries, span_kv, kv_store)
+    )(page_owner, page_ids, prefix_len, page_owner, queries, span_kv, kv_store)
 
 
 def solution(mesh):

time: 77.6 us -> 63.6 us (0.82)
  the two profiles are of different devices: /device:TPU:2 before, /device:TPU:1 now
where the time goes in v2:
time: 63.6 us; the launch traced here: 63.5 us
  Pallas kernels  60.5 us (95%)
  local copies, waits for them, and re-layouts  2.29 us (4%)
  between operations  0.66 us (1%)
    pallas_call x1, Pallas kernels, per_device(): pl.pallas_call(kernel, out_shape=jax.ShapeDtypeStruct(queries.shape, BF),...  60.5 us
    unnamed x1, local copies, waits for them, and re-layouts  2.29 us

profile of v2, /device:TPU:1, one launch (start us, length us, event | category | flops | bytes accessed | tf_op | source)
XLA Modules:
  0.0 63.5 jit_solution(12495505811050864663)
XLA Ops:
  0.7 60.5 %shard_map.64 = bf16[128,4096]{1,0:T(8,128)(2,1)} custom-call(s32[1,32]{1,0:T(1,128)} %own_v.1, s32[1,32]{1,0:T(1,128)} %ids_s.1, s32[1]{0:T(128)S(6)} %copy.8.len_s, s32[1,32]{1,0:T(1,128)} %own_v.1, bf16[128,4096]{1,0:T(8,128)(2,1)} %q_hbm.1, bf16[128,1024]{1,0:T(8,128)(2,1)} %span_hbm.1, bf16[16,64,1024]{2,1,0:T(8,128)(2,1)} %store_hbm.1), custom_call_target="tpu_custom_call" | custom-call | flops 6442450944 | bytes 4194304 | tf_op jit(solution)/shard_map/pallas_call | solution.py:469
  61.2 2.3 %copy.9 = bf16[128,4096]{1,0:T(8,128)(2,1)} copy(bf16[128,4096]{1,0:T(8,128)(2,1)} %shard_map.64) | data formatting | bytes 2097152

commit v3 on v2

--- a/solution.py
+++ b/solution.py
@@ -432,10 +432,11 @@
         8: [N(0)],
         12: [C(2)],
         16: [N(1), F(0)],
-        20: [C(3)],
+        18: [C(3)],
         24: [N(2), F(1)],
-        30: [N(3), F(2)],
-        38: [F(3)],
+        28: [N(3)],
+        30: [F(2)],
+        34: [F(3)],
     }
 
 

time: 63.6 us -> 63.1 us (level)
  no operation moved by 1% of the time
where the time goes in v3:
time: 63.1 us; the launch traced here: 62.9 us
  Pallas kernels  60 us (95%)
  local copies, waits for them, and re-layouts  2.29 us (4%)
  between operations  0.66 us (1%)
    pallas_call x1, Pallas kernels, per_device(): pl.pallas_call(kernel, out_shape=jax.ShapeDtypeStruct(queries.shape, BF),...  60 us
    unnamed x1, local copies, waits for them, and re-layouts  2.29 us

profile of v3, /device:TPU:1, one launch (start us, length us, event | category | flops | bytes accessed | tf_op | source)
XLA Modules:
  0.0 62.9 jit_solution(86498012881328357)
XLA Ops:
  0.7 60.0 %shard_map.64 = bf16[128,4096]{1,0:T(8,128)(2,1)} custom-call(s32[1,32]{1,0:T(1,128)} %own_v.1, s32[1,32]{1,0:T(1,128)} %ids_s.1, s32[1]{0:T(128)S(6)} %copy.8.len_s, s32[1,32]{1,0:T(1,128)} %own_v.1, bf16[128,4096]{1,0:T(8,128)(2,1)} %q_hbm.1, bf16[128,1024]{1,0:T(8,128)(2,1)} %span_hbm.1, bf16[16,64,1024]{2,1,0:T(8,128)(2,1)} %store_hbm.1), custom_call_target="tpu_custom_call" | custom-call | flops 6442450944 | bytes 4194304 | tf_op jit(solution)/shard_map/pallas_call | solution.py:470
  60.7 2.3 %copy.9 = bf16[128,4096]{1,0:T(8,128)(2,1)} copy(bf16[128,4096]{1,0:T(8,128)(2,1)} %shard_map.64) | data formatting | bytes 2097152
